TPU v7x, 32 devices: a whole 2x2x4 slice. The times are simulated.
32 devices in a mesh: group: 2 (over x), tm: 16 (over z, y, core).
Axes of the slice: x: 2, y: 2, z: 4, core: 2. Of those that a mesh axis runs over, the one named last changes fastest.
Arguments:
- obs_blocks: bfloat16 [32, 512, 64, 128], P(('group', 'tm')), parts along dimension 0, may hold values from -0.5 to 0.5
- block_rows: int32 [32, 512], P(('group', 'tm')), parts along dimension 0, may hold values from 0 to 511
- block_cols: int32 [32, 512], P(('group', 'tm')), parts along dimension 0, may hold values from 0 to 15
- block_count: int32 [32], P(('group', 'tm')), parts along dimension 0, may hold values from 256 to 512, as said below
- background: bfloat16 [32, 16, 2048], P(('group', 'tm')), parts along dimension 0, may hold values from -6 to 6
- observed: float32 [32, 16, 32768], P(('group', 'tm')), parts along dimension 0, may hold values from -6 to 6
- obs_weight: float32 [32, 32768], P(('group', 'tm')), parts along dimension 0, may hold values from 0.01 to 0.1
- info_diag: float32 [32, 2048], P(('group', 'tm')), parts along dimension 0, may hold values from 0.003 to 0.03
- decay: float32 [32, 2048], P(('group', 'tm')), parts along dimension 0, may hold values from 0.5 to 1
- noise_var: float32 [32, 2048], P(('group', 'tm')), parts along dimension 0, may hold values from 0.003 to 0.03
- prior_var: float32 [4096], P('group'), parts along dimension 0, may hold values from 0.5 to 2
Outputs:
- smooth_mean: float32 [32, 16, 2048], P(('group', 'tm')), parts along dimension 0
- smooth_var: float32 [32, 2048], P(('group', 'tm')), parts along dimension 0
There are 2 independent parts, one for each index of `group`. A program takes and returns all parts, laid end to end along the dimension named above; each array names one. Nothing has to cross between parts.
Inputs may be any that keep to these rules, and one draw needn't show every extreme that they name: Blocks 0 to block_count[t] - 1 of step t are in use; some step uses all 512 blocks and some step exactly half of them.
All inputs are finite; a program needn't handle non-finite values.
Results may differ from a plain program's by a relative error of at most 0.0045.
Values sent between devices are 32-bit elements; how exact they have to be, the bound alone decides.
A program may use at most 64 MiB of HBM per device.

v0:
```python
import jax
import jax.numpy as jnp
from jax import lax
from jax.sharding import PartitionSpec as P


def split_path(onehot, values, form):
    high_part = values.astype(jnp.bfloat16)
    rest_part = (values - high_part.astype(jnp.float32)).astype(jnp.bfloat16)
    first = jnp.einsum(form, onehot, high_part, preferred_element_type=jnp.float32)
    return first + jnp.einsum(form, onehot, rest_part, preferred_element_type=jnp.float32)


def gradients(obs_blocks, block_rows, block_cols, block_count, background, observed, obs_weight):
    step_total, block_total, row_size, col_size = obs_blocks.shape
    member_total = background.shape[1]
    group_total = background.shape[2] // col_size
    row_total = observed.shape[2] // row_size
    active = lax.broadcasted_iota(jnp.int32, (step_total, block_total), 1) < block_count[:, None]
    col_match = (
        block_cols[:, :, None]
        == lax.broadcasted_iota(jnp.int32, (step_total, block_total, group_total), 2)
    ).astype(jnp.bfloat16)
    row_match = block_rows[:, :, None] == lax.broadcasted_iota(
        jnp.int32, (step_total, block_total, row_total), 2
    )
    row_indicator = jnp.logical_and(row_match, active[:, :, None]).astype(jnp.bfloat16)
    states = background.reshape(step_total, member_total, group_total, col_size)
    picked = jnp.einsum(
        "sbk,smkc->smbc", col_match, states, preferred_element_type=jnp.float32
    ).astype(jnp.bfloat16)
    applied_result = jnp.einsum(
        "sbic,smbc->smbi", obs_blocks, picked, preferred_element_type=jnp.float32
    )
    mapped_images = split_path(row_indicator, applied_result, "dez,dwet->dwzt")
    misfit = observed - mapped_images.reshape(step_total, member_total, row_total * row_size)
    weighted = (obs_weight[:, None, :] * misfit).reshape(
        step_total, member_total, row_total, row_size
    )
    rows_back = jnp.einsum(
        "ocd,owdh->owch",
        row_indicator,
        weighted.astype(jnp.bfloat16),
        preferred_element_type=jnp.float32,
    ).astype(jnp.bfloat16)
    pulled = jnp.einsum(
        "sbic,smbi->smbc", obs_blocks, rows_back, preferred_element_type=jnp.float32
    )
    gradient = split_path(col_match, pulled, "sbk,smbc->smkc")
    return gradient.reshape(step_total, member_total, group_total * col_size)


def sequential_smoother(series, prior_here, member_total):
    full_steps = series.shape[0]
    grad_all = series[:, :member_total, :]
    info_all = series[:, member_total, :]
    decay_all = series[:, member_total + 1, :]
    noise_all = series[:, member_total + 2, :]
    local_width = series.shape[2]
    step_ids = jnp.arange(full_steps)
    first_flags = step_ids == 0
    final_flags = step_ids == full_steps - 1

    def forward(carried, inputs):
        mean_prev, var_prev = carried
        grad_now, info_now, decay_now, noise_now, first_now = inputs
        pred_var = jnp.where(first_now, prior_here, decay_now * decay_now * var_prev + noise_now)
        pred_mean = jnp.where(first_now, 0.0, decay_now * mean_prev)
        var_now = pred_var / (1.0 + info_now * pred_var)
        mean_now = var_now * (pred_mean / pred_var + grad_now)
        return ((mean_now, var_now), (mean_now, var_now))

    initial = (
        jnp.zeros((member_total, local_width), jnp.float32),
        jnp.ones((local_width,), jnp.float32),
    )
    means, variances = lax.scan(
        forward, initial, (grad_all, info_all, decay_all, noise_all, first_flags)
    )[1]
    next_decay = jnp.concatenate([decay_all[1:], jnp.zeros((1, local_width), jnp.float32)], axis=0)
    next_noise = jnp.concatenate([noise_all[1:], jnp.ones((1, local_width), jnp.float32)], axis=0)

    def backward(carried, inputs):
        later_mean, later_var = carried
        mean_now, var_now, decay_next, noise_next, final_now = inputs
        pred_var = decay_next * decay_next * var_now + noise_next
        smoother_gain = jnp.where(final_now, 0.0, var_now * decay_next / pred_var)
        out_mean = mean_now + smoother_gain * (later_mean - decay_next * mean_now)
        out_var = var_now + smoother_gain * smoother_gain * (later_var - pred_var)
        return ((out_mean, out_var), (out_mean, out_var))

    closing = (
        jnp.zeros((member_total, local_width), jnp.float32),
        jnp.zeros((local_width,), jnp.float32),
    )
    return lax.scan(
        backward, closing, (means, variances, next_decay, next_noise, final_flags), reverse=True
    )[1]


def shards(
    obs_blocks,
    block_rows,
    block_cols,
    block_count,
    background,
    observed,
    obs_weight,
    info_diag,
    decay,
    noise_var,
    prior_var,
):
    member_total = background.shape[1]
    state_total = background.shape[2]
    gradient = gradients(
        obs_blocks, block_rows, block_cols, block_count, background, observed, obs_weight
    )
    packed = jnp.concatenate(
        [gradient, info_diag[:, None, :], decay[:, None, :], noise_var[:, None, :]], axis=1
    )
    series = lax.all_to_all(packed, "tm", split_axis=2, concat_axis=0, tiled=True)
    local_width = state_total // lax.axis_size("tm")
    prior_here = lax.dynamic_slice_in_dim(
        prior_var, lax.axis_index("tm") * local_width, local_width, 0
    )
    mean_series, var_series = sequential_smoother(series, prior_here, member_total)
    outgoing = jnp.concatenate([mean_series, var_series[:, None, :]], axis=1)
    returned = lax.all_to_all(outgoing, "tm", split_axis=0, concat_axis=2, tiled=True)
    return (returned[:, :member_total, :], returned[:, member_total, :])


def solution(mesh):
    in_specs = (
        P(("group", "tm"), None, None, None),
        P(("group", "tm"), None),
        P(("group", "tm"), None),
        P(("group", "tm")),
        P(("group", "tm"), None, None),
        P(("group", "tm"), None, None),
        P(("group", "tm"), None),
        P(("group", "tm"), None),
        P(("group", "tm"), None),
        P(("group", "tm"), None),
        P("group"),
    )
    out_specs = (P(("group", "tm"), None, None), P(("group", "tm"), None))
    return jax.shard_map(shards, mesh=mesh, in_specs=in_specs, out_specs=out_specs, check_vma=False)
```

profile of v0, /device:TPU:0, one launch (start us, length us, event | category | flops | bytes accessed | tf_op | source)
XLA Modules:
  0.0 153.4 jit_solution(15889140871200153109)
XLA Ops:
  0.6 0.9 copy.100
  1.5 1.4 convert_bitcast_fusion
  2.9 7.2 %fusion.23 = f32[512,16,64]{2,1,0:T(8,128)S(1)} fusion(bf16[1,512,64,128]{3,2,1,0:T(8,128)(2,1)} %param.15, bf16[16,512,128]{2,1,0:T(8,128)(2,1)S(1)} %convert_bitcast_fusion), kind=kOutput, calls=%fused_computation.44 | convolution fusion | flops 134217728 | bytes 12582912 | tf_op jit(solution)/shard_map/sbic,smbc->smbi/dot_general | solution.py:32
  11.5 1.0 fusion.33
  12.5 1.1 add_bitcast_fusion
  13.6 2.7 %copy.84 = f32[1,16,512,64]{3,2,1,0:T(8,128)} copy(f32[1,16,512,64]{2,3,1,0:T(8,128)S(1)} %add_bitcast_fusion) | data formatting | bytes 4194304 | tf_op jit(solution)/shard_map/add | solution.py:11
  16.3 2.9 %reshape.249 = f32[1,16,32768]{2,1,0:T(8,128)S(1)} reshape(f32[1,16,512,64]{3,2,1,0:T(8,128)} %copy.84) | data formatting | bytes 4194304 | tf_op jit(solution)/shard_map/reshape | solution.py:36
  19.3 1.8 %multiply_convert_fusion = bf16[1,16,32768]{2,1,0:T(8,128)(2,1)S(1)} fusion(f32[1,16,32768]{2,1,0:T(8,128)} %param.20, f32[1,16,32768]{2,1,0:T(8,128)S(1)} %reshape.249, f32[32768]{0:T(1024)S(1)} %bitcast.211), kind=kLoop, calls=%fused_computation.63 | loop fusion | flops 1572864 | bytes 5373952 | tf_op jit(solution)/shard_map/convert_element_type | solution.py:43
  21.1 2.3 %convert_element_type.58 = bf16[16,512,64]{2,1,0:T(8,128)(2,1)S(1)} reshape(bf16[1,16,32768]{2,1,0:T(8,128)(2,1)S(1)} %multiply_convert_fusion) | data formatting | bytes 2097152 | tf_op jit(solution)/shard_map/convert_element_type | solution.py:43
  23.4 1.5 fusion.40
  24.9 2.0 %copy.86 = bf16[16,512,64]{2,0,1:T(8,128)(2,1)S(1)} copy(bf16[16,512,64]{1,2,0:T(8,128)(2,1)S(1)} %fusion.40) | data formatting | bytes 2097152 | tf_op jit(solution)/shard_map/reshape.26
  26.9 4.7 %fusion.21 = f32[512,16,128]{2,1,0:T(8,128)S(1)} fusion(bf16[16,512,64]{2,0,1:T(8,128)(2,1)S(1)} %copy.86, bf16[1,512,64,128]{3,2,1,0:T(8,128)(2,1)} %param.15), kind=kOutput, calls=%fused_computation.42 | convolution fusion | flops 134217728 | bytes 13631488 | tf_op jit(solution)/shard_map/sbic,smbi->smbc/dot_general | solution.py:46
  34.4 1.9 %copy.91 = f32[1,1,2048]{1,0,2:T(1,128)} copy(f32[1,1,2048]{2,1,0:T(1,128)S(1)} %bitcast.217) | data formatting | bytes 16384 | tf_op jit(solution)/shard_map/broadcast_in_dim | solution.py:120
  36.3 1.9 %copy.92 = f32[1,1,2048]{1,0,2:T(1,128)} copy(f32[1,1,2048]{2,1,0:T(1,128)S(1)} %bitcast.218) | data formatting | bytes 16384 | tf_op jit(solution)/shard_map/broadcast_in_dim | solution.py:120
  38.2 7.8 %fusion.69 = f32[2048,1,19]{2,1,0:T(1,128)S(1)} fusion(f32[1,1,2048]{1,0,2:T(1,128)} %copy.92, f32[1,1,2048]{1,0,2:T(1,128)} %copy.91, f32[1,1,2048]{1,0,2:T(1,128)S(1)} %copy.90, f32[1,16,2048]{1,0,2:T(1,128)S(1)} %bitcast.203), kind=kLoop, calls=%fused_computation.97 | loop fusion | flops 116736 | bytes 311296
  46.6 9.3 %reduce = f32[2048,19]{1,0:T(8,128)S(1)} reduce(f32[2048,1,19]{2,1,0:T(1,128)S(1)} %fusion.69, f32[]{:T(128)} %broadcast.158), dimensions={1}, to_apply=%fusion.69.reduce_sub_computation | reduce | bytes 311300
  55.8 1.5 reshape.256
  57.4 7.4 %all-to-all-start = ((f32[16,1,2432]{2,1,0:T(1,128)}), f32[16,1,2432]{2,1,0:T(1,128)S(1)}, u32[]{:S(2)}, u32[]{:S(2)}) async-start(f32[16,1,2432]{2,1,0:T(1,128)} %reshape.256), calls=%async_computation | async-start | bytes 311296 | tf_op jit(solution)/shard_map/all_to_all | solution.py:122
  65.6 7.5 %all-to-all-done = f32[16,1,2432]{2,1,0:T(1,128)S(1)} async-done(((f32[16,1,2432]{2,1,0:T(1,128)}), f32[16,1,2432]{2,1,0:T(1,128)S(1)}, u32[]{:S(2)}, u32[]{:S(2)}) %all-to-all-start) | async-done | bytes 155680 | tf_op jit(solution)/shard_map/all_to_all | solution.py:122
  73.1 0.9 reduce.1
  74.0 1.7 %reshape.257 = f32[2048,1,19]{2,1,0:T(1,128)S(1)} reshape(f32[16,2432]{1,0:T(8,128)S(1)} %reduce.1) | data formatting | bytes 311296
  76.4 31.9 %while.38 = (s32[]{:T(128)}, f32[16,128]{1,0:T(8,128)S(1)}, f32[128]{0:T(128)S(1)}, f32[16,16,128]{2,1,0:T(8,128)S(1)}, f32[16,128]{1,0:T(8,128)S(1)}, /*index=5...) while((s32[]{:T(128)}, f32[16,128]{1,0:T(8,128)S(1)}, ...), condition=%wide.region_1.2_spmd.clone, body=%wide.region_0.1_spmd.clone.sunk | while | flops 13315 | bytes 55968 | solution.py:77
  108.3 32.1 %while.39 = (s32[]{:T(128)}, f32[16,128]{1,0:T(8,128)S(1)}, f32[128]{0:T(128)S(1)}, f32[16,16,128]{2,1,0:T(8,128)S(1)}, f32[16,128]{1,0:T(8,128)S(1)}, /*index=5...) while((s32[]{:T(128)}, f32[16,128]{1,0:T(8,128)S(1)}, ...), condition=%wide.region_3.4_spmd.clone, body=%wide.region_2.3_spmd.clone.sunk | while | flops 12420 | bytes 40108 | solution.py:96
  140.4 11.6 %all_to_all.36 = f32[16,17,128]{2,1,0:T(8,128)S(1)} all-to-all(f32[16,17,128]{2,1,0:T(8,128)S(1)} %pad_maximum_fusion.1), channel_id=1, replica_groups=mesh['group'=2,'tm'=16] {'tm'}, dimensions={0} | all-to-all | bytes 278528 | tf_op jit(solution)/shard_map/all_to_all | solution.py:129
  (204 shorter events, 69.6 us)
Async XLA Ops:
  10.5 1.0 copy-start.4
  16.3 3.0 %copy-start = (f32[1,32768]{1,0:T(1,128)S(1)}, f32[1,32768]{1,0:T(1,128)}, u32[]{:S(2)}) copy-start(f32[1,32768]{1,0:T(1,128)} %param.21) | copy-start | bytes 393220
  31.9 0.7 copy-start.5
  33.0 0.8 copy-start.1
  33.0 1.4 copy-start.2
  33.4 2.9 %copy-start.3 = (f32[1,2048]{1,0:T(1,128)S(1)}, f32[1,2048]{1,0:T(1,128)}, u32[]{:S(2)}) copy-start(f32[1,2048]{1,0:T(1,128)} %param.24) | copy-start | bytes 24580
  57.4 15.7 %all-to-all-start = ((f32[16,1,2432]{2,1,0:T(1,128)}), f32[16,1,2432]{2,1,0:T(1,128)S(1)}, u32[]{:S(2)}, u32[]{:S(2)}) async-start(f32[16,1,2432]{2,1,0:T(1,128)} %reshape.256), calls=%async_computation | async-start | bytes 311296 | tf_op jit(solution)/shard_map/all_to_all | solution.py:122
where the time goes:
time: 154 us; the launch traced here: 153 us
  other arithmetic  63.4 us (41%)
  local copies, waits for them, and re-layouts  43.1 us (28%)
  matrix products  17.7 us (11%)
  blocking collectives  11.6 us (8%)
  waiting for transfers between devices  7.51 us (5%)
  starting transfers between devices  7.39 us (5%)
  between operations  1.64 us (1%)
    dynamic_slice x48, local copies, waits for them, and re-layouts, sequential_smoother(): lax.scan(forward, initial, (grad_all, info_all, decay_all, noise_all, fir...  19.5 us
    unnamed x6, other arithmetic  17.1 us
    all_to_all x1, blocking collectives, shards(): lax.all_to_all(outgoing, 'tm', split_axis=0, concat_axis=2, tiled=True)  11.6 us
    add x16, other arithmetic, backward(): out_var = var_now + smoother_gain * smoother_gain * (later_var - pred_var)  10.7 us
    mul x16, other arithmetic, backward(): out_mean = mean_now + smoother_gain * (later_mean - decay_next * mean_now)  10.5 us
    dynamic_update_slice x32, other arithmetic, sequential_smoother(): lax.scan(forward, initial, (grad_all, info_all, decay_all, noise_all, fir...  10.5 us
    div x16, other arithmetic, forward(): var_now = pred_var / (1.0 + info_now * pred_var)  10.5 us
    all_to_all x1, waiting for transfers between devices, shards(): lax.all_to_all(packed, 'tm', split_axis=2, concat_axis=0, tiled=True)  7.51 us
  transfers between devices with their start and end apart: 1, of which 1 were waited for; matrix products, arithmetic and copies ran while one was open for 1% of the time, Pallas kernels for 0%

commit v1 on v0

--- a/solution.py
+++ b/solution.py
@@ -119,7 +119,10 @@
     packed = jnp.concatenate(
         [gradient, info_diag[:, None, :], decay[:, None, :], noise_var[:, None, :]], axis=1
     )
-    series = lax.all_to_all(packed, "tm", split_axis=2, concat_axis=0, tiled=True)
+    series = jnp.concatenate(
+        lax.all_to_all(jnp.stack(jnp.split(packed, lax.axis_size("tm"), axis=2)), "tm", 0, 0),
+        axis=0,
+    )
     local_width = state_total // lax.axis_size("tm")
     prior_here = lax.dynamic_slice_in_dim(
         prior_var, lax.axis_index("tm") * local_width, local_width, 0

time: 154 us -> 137 us (0.89)
  other arithmetic: 63.4 us -> 45.1 us
    unnamed x6 -> x4, other arithmetic: 17.1 us -> 0.01 us
    unnamed x16 -> x28, local copies, waits for them, and re-layouts: 4.97 us -> 10.3 us
    broadcast_in_dim x3 -> x0, local copies, waits for them, and re-layouts: 4.43 us -> none  [the longest x1 1.92 us: shards(): decay[:, None, :]]
where the time goes in v1:
time: 137 us; the launch traced here: 136 us
  other arithmetic  45.1 us (33%)
  local copies, waits for them, and re-layouts  44.3 us (32%)
  matrix products  17.9 us (13%)
  blocking collectives  11.6 us (8%)
  waiting for transfers between devices  7.51 us (5%)
  starting transfers between devices  7.39 us (5%)
  between operations  1.6 us (1%)
    dynamic_slice x48, local copies, waits for them, and re-layouts, sequential_smoother(): lax.scan(forward, initial, (grad_all, info_all, decay_all, noise_all, fir...  20.1 us
    all_to_all x1, blocking collectives, shards(): lax.all_to_all(outgoing, 'tm', split_axis=0, concat_axis=2, tiled=True)  11.6 us
    add x16, other arithmetic, backward(): out_var = var_now + smoother_gain * smoother_gain * (later_var - pred_var)  10.7 us
    mul x16, other arithmetic, backward(): out_mean = mean_now + smoother_gain * (later_mean - decay_next * mean_now)  10.5 us
    dynamic_update_slice x32, other arithmetic, sequential_smoother(): lax.scan(forward, initial, (grad_all, info_all, decay_all, noise_all, fir...  10.3 us
    unnamed x28, local copies, waits for them, and re-layouts  10.3 us
    div x16, other arithmetic, forward(): var_now = pred_var / (1.0 + info_now * pred_var)  10.3 us
    all_to_all x1, waiting for transfers between devices, shards(): lax.all_to_all(jnp.stack(jnp.split(packed, lax.axis_size('tm'), axis=2)),...  7.51 us
  transfers between devices with their start and end apart: 1, of which 1 were waited for; matrix products, arithmetic and copies ran while one was open for 1% of the time, Pallas kernels for 0%

profile of v1, /device:TPU:0, one launch (start us, length us, event | category | flops | bytes accessed | tf_op | source)
XLA Modules:
  0.0 136.4 jit_solution(16512214551454644555)
XLA Ops:
  0.6 0.9 copy.102
  1.5 1.4 %convert_bitcast_fusion = bf16[16,512,128]{2,1,0:T(8,128)(2,1)S(1)} fusion(bf16[16,16,128]{2,1,0:T(8,128)(2,1)S(1)} %bitcast.297, s32[512]{0:T(512)} %bitcast.310), kind=kOutput, calls=%fused_computation.65 | convolution fusion | flops 34611200 | bytes 2164736 | tf_op jit(solution)/shard_map/sbk,smkc->smbc/dot_general | solution.py:29
  2.9 7.2 %fusion.23 = f32[512,16,64]{2,1,0:T(8,128)S(1)} fusion(bf16[1,512,64,128]{3,2,1,0:T(8,128)(2,1)} %param.15, bf16[16,512,128]{2,1,0:T(8,128)(2,1)S(1)} %convert_bitcast_fusion), kind=kOutput, calls=%fused_computation.44 | convolution fusion | flops 134217728 | bytes 12582912 | tf_op jit(solution)/shard_map/sbic,smbc->smbi/dot_general | solution.py:32
  11.5 1.0 fusion.33
  12.5 1.1 add_bitcast_fusion
  13.6 2.7 %copy.75 = f32[1,16,512,64]{3,2,1,0:T(8,128)} copy(f32[1,16,512,64]{2,3,1,0:T(8,128)S(1)} %add_bitcast_fusion) | data formatting | bytes 4194304 | tf_op jit(solution)/shard_map/add | solution.py:11
  16.3 2.9 %reshape.252 = f32[1,16,32768]{2,1,0:T(8,128)S(1)} reshape(f32[1,16,512,64]{3,2,1,0:T(8,128)} %copy.75) | data formatting | bytes 4194304 | tf_op jit(solution)/shard_map/reshape | solution.py:36
  19.3 1.8 %multiply_convert_fusion = bf16[1,16,32768]{2,1,0:T(8,128)(2,1)S(1)} fusion(f32[1,16,32768]{2,1,0:T(8,128)} %param.20, f32[1,16,32768]{2,1,0:T(8,128)S(1)} %reshape.252, f32[32768]{0:T(1024)S(1)} %bitcast.299), kind=kLoop, calls=%fused_computation.63 | loop fusion | flops 1572864 | bytes 5373952 | tf_op jit(solution)/shard_map/convert_element_type | solution.py:43
  21.1 2.3 %convert_element_type.58 = bf16[16,512,64]{2,1,0:T(8,128)(2,1)S(1)} reshape(bf16[1,16,32768]{2,1,0:T(8,128)(2,1)S(1)} %multiply_convert_fusion) | data formatting | bytes 2097152 | tf_op jit(solution)/shard_map/convert_element_type | solution.py:43
  23.4 1.5 %fusion.40 = bf16[16,512,64]{1,2,0:T(8,128)(2,1)S(1)} fusion(bf16[16,512,64]{2,1,0:T(8,128)(2,1)S(1)} %convert_element_type.58, s32[512]{0:T(512)S(1)} %bitcast.306, pred[512]{0:T(512)(128)(4,1)S(1)} %iota_compare_fusion.2), kind=kOutput, calls=%fused_computation.67 | convolution fusion | flops 537919488 | bytes 2099712 | tf_op jit(solution)/shard_map/ocd,owdh->owch/dot_general | solution.py:40
  24.9 2.0 %copy.77 = bf16[16,512,64]{2,0,1:T(8,128)(2,1)S(1)} copy(bf16[16,512,64]{1,2,0:T(8,128)(2,1)S(1)} %fusion.40) | data formatting | bytes 2097152 | tf_op jit(solution)/shard_map/reshape.27
  26.9 4.9 %fusion.21 = f32[512,16,128]{2,1,0:T(8,128)S(1)} fusion(bf16[16,512,64]{2,0,1:T(8,128)(2,1)S(1)} %copy.77, bf16[1,512,64,128]{3,2,1,0:T(8,128)(2,1)} %param.15), kind=kOutput, calls=%fused_computation.42 | convolution fusion | flops 134217728 | bytes 13631488 | tf_op jit(solution)/shard_map/sbic,smbi->smbc/dot_general | solution.py:46
  43.4 7.4 %all-to-all-start = ((f32[16,1,19,128]{3,1,2,0:T(1,128)}), f32[16,1,19,128]{3,1,2,0:T(1,128)S(1)}, u32[]{:S(2)}, u32[]{:S(2)}) async-start(f32[16,1,19,128]{3,1,2,0:T(1,128)} %constant_dynamic-update-slice_fusion), calls=%async_computation | async-start | bytes 311296 | tf_op jit(solution)/shard_map/all_to_all | solution.py:123
  50.9 0.8 dynamic_slice.66
  51.6 7.5 %all-to-all-done = f32[16,1,19,128]{3,1,2,0:T(1,128)S(1)} async-done(((f32[16,1,19,128]{3,1,2,0:T(1,128)}), f32[16,1,19,128]{3,1,2,0:T(1,128)S(1)}, u32[]{:S(2)}, u32[]{:S(2)}) %all-to-all-start) | async-done | bytes 155680 | tf_op jit(solution)/shard_map/all_to_all | solution.py:123
  59.2 32.0 %while.38 = (s32[]{:T(128)}, f32[16,128]{1,0:T(8,128)S(1)}, f32[128]{0:T(128)S(1)}, f32[16,16,128]{2,1,0:T(8,128)S(1)}, f32[16,128]{1,0:T(8,128)S(1)}, /*index=5...) while((s32[]{:T(128)}, f32[16,128]{1,0:T(8,128)S(1)}, ...), condition=%wide.region_1.2_spmd.clone, body=%wide.region_0.1_spmd.clone.sunk | while | flops 13315 | bytes 55968 | solution.py:77
  91.3 32.1 %while.39 = (s32[]{:T(128)}, f32[16,128]{1,0:T(8,128)S(1)}, f32[128]{0:T(128)S(1)}, f32[16,16,128]{2,1,0:T(8,128)S(1)}, f32[16,128]{1,0:T(8,128)S(1)}, /*index=5...) while((s32[]{:T(128)}, f32[16,128]{1,0:T(8,128)S(1)}, ...), condition=%wide.region_3.4_spmd.clone, body=%wide.region_2.3_spmd.clone.sunk | while | flops 12420 | bytes 40108 | solution.py:96
  92.6 0.7 fusion.74
  94.6 0.7 fusion.74
  96.6 0.7 fusion.74
  100.6 0.7 fusion.74
  102.7 0.7 fusion.74
  104.7 0.7 fusion.74
  123.4 11.6 %all_to_all.23 = f32[16,17,128]{2,1,0:T(8,128)S(1)} all-to-all(f32[16,17,128]{2,1,0:T(8,128)S(1)} %pad_maximum_fusion), channel_id=1, replica_groups=mesh['group'=2,'tm'=16] {'tm'}, dimensions={0} | all-to-all | bytes 278528 | tf_op jit(solution)/shard_map/all_to_all | solution.py:132
  (211 shorter events, 72.7 us)
Async XLA Ops:
  10.5 1.0 copy-start.1
  16.3 3.0 %copy-start = (f32[1,32768]{1,0:T(1,128)S(1)}, f32[1,32768]{1,0:T(1,128)}, u32[]{:S(2)}) copy-start(f32[1,32768]{1,0:T(1,128)} %param.21) | copy-start | bytes 393220
  32.1 0.7 copy-start.5
  32.8 0.8 copy-start.2
  32.8 0.8 copy-start.3
  32.8 0.8 copy-start.4
  43.4 15.7 %all-to-all-start = ((f32[16,1,19,128]{3,1,2,0:T(1,128)}), f32[16,1,19,128]{3,1,2,0:T(1,128)S(1)}, u32[]{:S(2)}, u32[]{:S(2)}) async-start(f32[16,1,19,128]{3,1,2,0:T(1,128)} %constant_dynamic-update-slice_fusion), calls=%async_computation | async-start | bytes 311296 | tf_op jit(solution)/shard_map/all_to_all | solution.py:123
